TPU v7x, 128 devices: a whole 4x4x4 slice. The times are simulated.
128 devices in a mesh: section: 8 (over x, z_lo), work: 16 (over y, z_hi, core).
Axes of the slice: x: 4, y: 4, z: 4 (z_hi: 2, z_lo: 2; z = z_hi * 2 + z_lo), core: 2. Of those that a mesh axis runs over, the one named last changes fastest.
Arguments:
- queries: bfloat16 [8, 8192, 4096], P('section', 'work')
- new_keys: bfloat16 [8, 8192, 512], P('section', 'work')
- new_values: bfloat16 [8, 8192, 512], P('section', 'work'), may hold values from -6 to 6
- cache_keys: bfloat16 [8, 256, 128, 512], P('section', 'work'), may hold values from -6 to 6
- cache_values: bfloat16 [8, 256, 128, 512], P('section', 'work'), may hold values from -6 to 6
- block_ids: int32 [8, 16, 4], P('section'), may hold values from 0 to 255, as said below
- block_counts: int32 [8, 16], P('section'), may hold values from 3 to 4
Outputs:
- handed: bfloat16 [8, 8192, 4096], P('section', 'work')
Inputs may be any that keep to these rules, and one draw needn't show every extreme that they name: `block_ids`: block id b of a section lies on the device of index b // 16 along work; the first block_counts entries of a list are its prefix, the rest are ignored; the ids of one list lie on different devices.
All inputs are finite; a program needn't handle non-finite values.
Results may differ from a plain program's by a relative error of at most 0.006.
Values may be sent and summed in bfloat16 or wider, within the bound.
A program may use at most 192 MiB of HBM per device.

v0:
```python
import jax
import jax.numpy as jnp
from jax import lax
from jax.sharding import PartitionSpec as P

HD = 128


masked_score = -1e30


def from_behind(block, axis, distance):
    devices = range(lax.axis_size(axis))
    route = [((i - distance) % len(devices), i) for i in devices]
    return lax.ppermute(block, axis, route)


def absorb(state, scores, value_block, heads_kv):
    running, totals, accumulated = state
    fresh_peak = jnp.maximum(running, jnp.max(scores, -1))
    rescale = jnp.exp(running - fresh_peak)
    weights = jnp.exp(scores - fresh_peak[..., None])
    totals = totals * rescale + jnp.sum(weights, -1)
    values = value_block.reshape(value_block.shape[0], heads_kv, HD)
    update = jnp.einsum(
        "kgct,tkd->kgcd", weights.astype(jnp.bfloat16), values, preferred_element_type=jnp.float32
    )
    return (fresh_peak, totals, accumulated * rescale[..., None] + update)


def start_state(tokens, heads_kv, groups):
    return (
        jnp.full((heads_kv, groups, tokens), masked_score, jnp.float32),
        jnp.zeros((heads_kv, groups, tokens), jnp.float32),
        jnp.zeros((heads_kv, groups, tokens, HD), jnp.float32),
    )


def local_part(state, grouped, fresh_keys, fresh_values, heads_kv):
    tokens = grouped.shape[0]
    own_keys = fresh_keys.reshape(tokens, heads_kv, HD)
    scores = jnp.einsum(
        "ckgd,tkd->kgct", grouped, own_keys, preferred_element_type=jnp.float32
    ) * HD ** (-0.5)
    positions = jnp.arange(tokens)
    scores = jnp.where(positions[None, :] <= positions[:, None], scores, masked_score)
    return absorb(state, scores, fresh_values, heads_kv)


def prefix_part(state, grouped, prefix_keys, prefix_values, prefix_count, heads_kv):
    block_rows = prefix_keys.shape[1]

    def visit(position, carried):
        key_block = lax.dynamic_index_in_dim(prefix_keys, position, 0, keepdims=False)
        key_block = key_block.reshape(block_rows, heads_kv, HD)
        value_block = lax.dynamic_index_in_dim(prefix_values, position, 0, keepdims=False)
        scores = jnp.einsum(
            "ckgd,tkd->kgct", grouped, key_block, preferred_element_type=jnp.float32
        ) * HD ** (-0.5)
        return absorb(carried, scores, value_block, heads_kv)

    return lax.fori_loop(0, prefix_count, visit, state)


def finish(state, tokens):
    running, totals, accumulated = state
    mixed_heads = accumulated / totals[..., None]
    return jnp.transpose(mixed_heads, (2, 0, 1, 3)).reshape(tokens, -1).astype(jnp.bfloat16)


def shards(queries, new_keys, new_values, cache_keys, cache_values, block_ids, block_counts):
    own_index = lax.axis_index("work")
    held = cache_keys.shape[1]
    block_list = block_ids[0]
    counts = block_counts[0]
    listed = block_list.shape[1]
    active = jnp.arange(listed)[None, :] < counts[:, None]
    matched = active & (block_list // held == own_index)
    present = jnp.any(matched, 1)
    local_slot = jnp.sum(jnp.where(matched, block_list % held, 0), 1)
    blank = jnp.zeros((), jnp.bfloat16)
    query_rows = queries[0]
    fresh_keys = new_keys[0]
    fresh_values = new_values[0]
    tokens = query_rows.shape[0]
    heads_kv = fresh_keys.shape[1] // HD
    groups = query_rows.shape[1] // HD // heads_kv
    grouped = query_rows.reshape(tokens, heads_kv, groups, HD)
    initial = start_state(tokens, heads_kv, groups)
    own_list = lax.dynamic_index_in_dim(block_list, own_index, 0, keepdims=False)
    own_count = lax.dynamic_index_in_dim(counts, own_index, 0, keepdims=False)
    holders = own_list // held
    state = initial
    outgoing_keys = jnp.where(present[:, None, None], cache_keys[0][local_slot], blank)
    outgoing_values = jnp.where(present[:, None, None], cache_values[0][local_slot], blank)
    arrived_keys, arrived_values = (
        lax.all_to_all(outgoing_keys, "work", split_axis=0, concat_axis=0, tiled=True),
        lax.all_to_all(outgoing_values, "work", split_axis=0, concat_axis=0, tiled=True),
    )
    prefix_keys = arrived_keys[holders]
    prefix_values = arrived_values[holders]
    state = prefix_part(state, grouped, prefix_keys, prefix_values, own_count, heads_kv)
    state = local_part(state, grouped, fresh_keys, fresh_values, heads_kv)
    context = finish(state, tokens)
    return from_behind(context[None], "section", 1)


def solution(mesh):
    in_specs = (
        P("section", "work", None),
        P("section", "work", None),
        P("section", "work", None),
        P("section", "work", None, None),
        P("section", "work", None, None),
        P("section", None, None),
        P("section", None),
    )
    out_specs = P("section", "work", None)
    return jax.shard_map(shards, mesh=mesh, in_specs=in_specs, out_specs=out_specs, check_vma=False)
```

profile of v0, /device:TPU:72, one launch (start us, length us, event | category | flops | bytes accessed | tf_op | source)
XLA Modules:
  0.0 312.1 jit_solution(11746594588030550214)
XLA Ops:
  0.0 0.0 copy-start
  0.0 0.9 fusion.30
  0.9 0.7 fusion.22
  1.6 0.0 copy-done
  1.6 2.0 gather_fusion.2
  3.6 2.3 gather_fusion
  5.9 0.0 copy-start.6
  5.9 0.0 copy-start.5
  5.9 3.3 %broadcast_select_fusion = (bf16[16,128,512]{2,1,0:T(8,128)(2,1)}, bf16[16,128,512]{2,1,0:T(8,128)(2,1)S(1)}) fusion(bf16[16,128,512]{2,1,0:T(8,128)(2,1)} %gather_fusion.2, pred[16]{0:T(512)(128)(4,1)S(1)} %get-tuple-element.89, bf16[16,128,512]{2,1,0:T(8,128)(2,1)S(1)} %gather_fusion), kind=kLoop, calls=%fused_computation.26 | loop fusion | flops 2097152 | bytes 8388624 | tf_op jit(solution)/shard_map/jit(_where)/select_n | solution.py:95
  9.2 31.7 %all_to_all.10 = bf16[16,128,512]{2,1,0:T(8,128)(2,1)} all-to-all(bf16[16,128,512]{2,1,0:T(8,128)(2,1)S(1)} %get-tuple-element.96), channel_id=1, replica_groups=mesh['section'=8,'work'=16] {'work'}, dimensions={0} | all-to-all | bytes 4194304 | tf_op jit(solution)/shard_map/all_to_all | solution.py:97
  40.9 9.0 %all-to-all-start.1 = ((bf16[16,128,512]{2,1,0:T(8,128)(2,1)}), bf16[16,128,512]{2,1,0:T(8,128)(2,1)}, u32[]{:S(2)}, u32[]{:S(2)}) async-start(bf16[16,128,512]{2,1,0:T(8,128)(2,1)} %get-tuple-element.95), calls=%async_computation.1 | async-start | bytes 4194304 | tf_op jit(solution)/shard_map/all_to_all | solution.py:98
  49.9 0.0 copy-done.6
  49.9 0.6 constant_dynamic-slice_fusion.2
  50.5 0.0 copy-done.5
  50.5 0.2 dynamic-slice_reduce_fusion
  50.7 0.0 copy-start.4
  50.7 6.5 %copy.28 = bf16[1,512,4096]{1,2,0:T(8,128)(2,1)} copy(bf16[1,512,4096]{2,1,0:T(8,128)(2,1)} %param.9) | data formatting | bytes 8388608 | tf_op args[0]
  57.2 6.2 %copy.30 = bf16[512,4,8,128]{3,0,2,1:T(8,128)(2,1)} copy(bf16[512,4,8,128]{0,3,2,1:T(8,128)(2,1)} %bitcast.110) | data formatting | bytes 8388608 | tf_op jit(solution)/shard_map/while | solution.py:62
  63.4 0.0 copy-done.3
  63.4 0.1 reshape_squeeze.10
  63.5 0.0 copy-done.4
  63.5 0.2 copy.51
  63.7 0.1 iota_compare_fusion
  63.8 16.1 %fusion.12 = (f32[4,8,512]{2,1,0:T(8,128)S(1)}, f32[4,512,512,8]{2,1,3,0:T(8,128)}) fusion(pred[512,512]{0,1:T(8,128)(4,1)S(1)} %iota_compare_fusion, bf16[512,4,8,128]{0,3,2,1:T(8,128)(2,1)} %bitcast.111, bf16[512,4,128,1]{2,1,0,3:T(4,128)(2,1)S(1)} %bitcast.115), kind=kOutput, calls=%fused_computation.22 | convolution fusion | flops 2172633088 | bytes 38600704 | tf_op jit(solution)/shard_map/ckgd,tkd->kgct/dot_general | solution.py:42
  79.9 2.2 gather_fusion.1
  82.1 0.0 all-to-all-done.1
  82.1 2.2 gather_fusion.3
  84.3 4.2 %broadcast_in_dim.52 = f32[4,8,512,128]{3,2,1,0:T(8,128)} broadcast(f32[]{:T(128)} %constant.76.clone.1), dimensions={} | broadcast | bytes 8388612 | tf_op jit(solution)/shard_map/broadcast_in_dim | solution.py:35
  88.4 77.3 %while.14 = (s32[]{:T(128)}, f32[4,8,512]{2,1,0:T(8,128)S(1)}, f32[4,8,512]{2,1,0:T(8,128)S(1)}, f32[4,8,512,128]{3,2,1,0:T(8,128)}, s32[]{:T(128)}, /*index=5*/...) while((s32[]{:T(128)}, f32[4,8,512]{2,1,0:T(8,128)S(1)}, ...), condition=%wide.region_5.6_spmd, body=%wide.region_2.5_spmd.sunk | while | flops 1094746112 | bytes 82051256 | solution.py:62
  89.1 0.1 copy.60
  89.2 3.5 %bitcast_reduce_fusion.2 = (f32[4,8,512]{2,1,0:T(8,128)S(1)}, f32[4,128,512,8]{2,1,3,0:T(8,128)S(1)}) fusion(bf16[128,4,128,1]{0,2,3,1:T(8,128)(2,1)S(1)} %bitcast.113, bf16[512,4,8,128]{3,0,2,1:T(8,128)(2,1)} %get-tuple-element.189), kind=kOutput, calls=%fused_computation.5.clone.1 | convolution fusion | flops 541048832 | bytes 12779520 | tf_op jit(solution)/shard_map/while/body/ckgd,tkd->kgct/dot_general | solution.py:57
  92.7 0.0 copy-start.2
  92.7 3.2 %copy-done.2 = f32[4,128,512,8]{2,1,3,0:T(8,128)} copy-done((f32[4,128,512,8]{2,1,3,0:T(8,128)}, f32[4,128,512,8]{2,1,3,0:T(8,128)S(1)}, u32[]{:S(2)}) %copy-start.2) | copy-done | bytes 8388632 | tf_op jit(solution)/shard_map/while
  95.9 1.7 fusion.46
  97.7 0.1 copy.61
  97.8 9.8 %multiply_add_fusion.6 = f32[4,8,512,128]{3,2,1,0:T(8,128)} fusion(f32[4,8,512,128]{3,2,1,0:T(8,128)} %get-tuple-element.175, f32[4,8,512]{2,1,0:T(8,128)S(1)} %get-tuple-element.159, bf16[128,4,128,1]{0,2,3,1:T(8,128)(2,1)S(1)} %bitcast.112, f32[4,128,512,8]{2,1,3,0:T(8,128)} %copy-done.2, f32[4,8,512]{2,1,0:T(8,128)S(1)} %max.8), kind=kOutput, calls=%fused_computation.7.clone.1 | convolution fusion | flops 547356672 | bytes 25427968 | tf_op jit(solution)/shard_map/while/body/kgct,tkd->kgcd/dot_general | solution.py:25
  108.2 0.1 copy.60
  108.3 3.5 %bitcast_reduce_fusion.2 = (f32[4,8,512]{2,1,0:T(8,128)S(1)}, f32[4,128,512,8]{2,1,3,0:T(8,128)S(1)}) fusion(bf16[128,4,128,1]{0,2,3,1:T(8,128)(2,1)S(1)} %bitcast.113, bf16[512,4,8,128]{3,0,2,1:T(8,128)(2,1)} %get-tuple-element.189), kind=kOutput, calls=%fused_computation.5.clone.1 | convolution fusion | flops 541048832 | bytes 12779520 | tf_op jit(solution)/shard_map/while/body/ckgd,tkd->kgct/dot_general | solution.py:57
  111.8 0.0 copy-start.2
  111.9 3.2 %copy-done.2 = f32[4,128,512,8]{2,1,3,0:T(8,128)} copy-done((f32[4,128,512,8]{2,1,3,0:T(8,128)}, f32[4,128,512,8]{2,1,3,0:T(8,128)S(1)}, u32[]{:S(2)}) %copy-start.2) | copy-done | bytes 8388632 | tf_op jit(solution)/shard_map/while
  115.0 1.7 fusion.46
  116.8 0.1 copy.61
  116.9 9.8 %multiply_add_fusion.6 = f32[4,8,512,128]{3,2,1,0:T(8,128)} fusion(f32[4,8,512,128]{3,2,1,0:T(8,128)} %get-tuple-element.175, f32[4,8,512]{2,1,0:T(8,128)S(1)} %get-tuple-element.159, bf16[128,4,128,1]{0,2,3,1:T(8,128)(2,1)S(1)} %bitcast.112, f32[4,128,512,8]{2,1,3,0:T(8,128)} %copy-done.2, f32[4,8,512]{2,1,0:T(8,128)S(1)} %max.8), kind=kOutput, calls=%fused_computation.7.clone.1 | convolution fusion | flops 547356672 | bytes 25427968 | tf_op jit(solution)/shard_map/while/body/kgct,tkd->kgcd/dot_general | solution.py:25
  127.3 0.1 copy.60
  127.5 3.5 %bitcast_reduce_fusion.2 = (f32[4,8,512]{2,1,0:T(8,128)S(1)}, f32[4,128,512,8]{2,1,3,0:T(8,128)S(1)}) fusion(bf16[128,4,128,1]{0,2,3,1:T(8,128)(2,1)S(1)} %bitcast.113, bf16[512,4,8,128]{3,0,2,1:T(8,128)(2,1)} %get-tuple-element.189), kind=kOutput, calls=%fused_computation.5.clone.1 | convolution fusion | flops 541048832 | bytes 12779520 | tf_op jit(solution)/shard_map/while/body/ckgd,tkd->kgct/dot_general | solution.py:57
  131.0 0.0 copy-start.2
  131.0 3.2 %copy-done.2 = f32[4,128,512,8]{2,1,3,0:T(8,128)} copy-done((f32[4,128,512,8]{2,1,3,0:T(8,128)}, f32[4,128,512,8]{2,1,3,0:T(8,128)S(1)}, u32[]{:S(2)}) %copy-start.2) | copy-done | bytes 8388632 | tf_op jit(solution)/shard_map/while
  134.2 1.7 fusion.46
  135.9 0.1 copy.61
  136.1 9.8 %multiply_add_fusion.6 = f32[4,8,512,128]{3,2,1,0:T(8,128)} fusion(f32[4,8,512,128]{3,2,1,0:T(8,128)} %get-tuple-element.175, f32[4,8,512]{2,1,0:T(8,128)S(1)} %get-tuple-element.159, bf16[128,4,128,1]{0,2,3,1:T(8,128)(2,1)S(1)} %bitcast.112, f32[4,128,512,8]{2,1,3,0:T(8,128)} %copy-done.2, f32[4,8,512]{2,1,0:T(8,128)S(1)} %max.8), kind=kOutput, calls=%fused_computation.7.clone.1 | convolution fusion | flops 547356672 | bytes 25427968 | tf_op jit(solution)/shard_map/while/body/kgct,tkd->kgcd/dot_general | solution.py:25
  146.5 0.1 copy.60
  146.6 3.5 %bitcast_reduce_fusion.2 = (f32[4,8,512]{2,1,0:T(8,128)S(1)}, f32[4,128,512,8]{2,1,3,0:T(8,128)S(1)}) fusion(bf16[128,4,128,1]{0,2,3,1:T(8,128)(2,1)S(1)} %bitcast.113, bf16[512,4,8,128]{3,0,2,1:T(8,128)(2,1)} %get-tuple-element.189), kind=kOutput, calls=%fused_computation.5.clone.1 | convolution fusion | flops 541048832 | bytes 12779520 | tf_op jit(solution)/shard_map/while/body/ckgd,tkd->kgct/dot_general | solution.py:57
  150.1 0.0 copy-start.2
  150.1 3.2 %copy-done.2 = f32[4,128,512,8]{2,1,3,0:T(8,128)} copy-done((f32[4,128,512,8]{2,1,3,0:T(8,128)}, f32[4,128,512,8]{2,1,3,0:T(8,128)S(1)}, u32[]{:S(2)}) %copy-start.2) | copy-done | bytes 8388632 | tf_op jit(solution)/shard_map/while
  153.3 1.7 fusion.46
  155.1 0.1 copy.61
  155.2 9.8 %multiply_add_fusion.6 = f32[4,8,512,128]{3,2,1,0:T(8,128)} fusion(f32[4,8,512,128]{3,2,1,0:T(8,128)} %get-tuple-element.175, f32[4,8,512]{2,1,0:T(8,128)S(1)} %get-tuple-element.159, bf16[128,4,128,1]{0,2,3,1:T(8,128)(2,1)S(1)} %bitcast.112, f32[4,128,512,8]{2,1,3,0:T(8,128)} %copy-done.2, f32[4,8,512]{2,1,0:T(8,128)S(1)} %max.8), kind=kOutput, calls=%fused_computation.7.clone.1 | convolution fusion | flops 547356672 | bytes 25427968 | tf_op jit(solution)/shard_map/while/body/kgct,tkd->kgcd/dot_general | solution.py:25
  165.7 8.7 %copy.34 = f32[4,8,512,128]{2,3,1,0:T(8,128)} copy(f32[4,8,512,128]{3,2,1,0:T(8,128)} %get-tuple-element.50) | data formatting | bytes 16777216 | tf_op jit(solution)/shard_map/while | solution.py:62
  174.4 14.6 %fusion.10 = f32[4,8,512]{2,1,0:T(8,128)S(1)} fusion(f32[4,512,512,8]{2,1,3,0:T(8,128)} %get-tuple-element.98, f32[4,8,512]{2,1,0:T(8,128)S(1)} %max.6, pred[512,512]{0,1:T(8,128)(4,1)S(1)} %iota_compare_fusion), kind=kLoop, calls=%fused_computation.20 | loop fusion | flops 33538048 | bytes 33947648 | tf_op jit(solution)/shard_map/reduce_sum | solution.py:23
  189.0 19.6 %divide_convert_fusion = bf16[4,8,512,128]{2,3,1,0:T(8,128)(2,1)} fusion(f32[4,8,512,128]{2,3,1,0:T(8,128)} %copy.34, f32[4,8,512]{2,1,0:T(8,128)S(1)} %get-tuple-element.87, f32[4,8,512]{2,1,0:T(8,128)S(1)} %get-tuple-element.88, bf16[512,4,128,1]{0,2,3,1:T(8,128)(2,1)S(1)} %bitcast.117, f32[4,512,512,8]{2,1,3,0:T(8,128)} %get-tuple-element.98, ...), kind=kOutput, calls=%fused_computation.25 | convolution fusion | flops 2189426688 | bytes 47120384 | tf_op jit(solution)/shard_map/kgct,tkd->kgcd/dot_general | solution.py:25
  208.6 6.6 %copy.37 = bf16[1,512,4096]{2,1,0:T(8,128)(2,1)} copy(bf16[1,512,4096]{1,2,0:T(8,128)(2,1)} %bitcast.114) | data formatting | bytes 8388608 | tf_op jit(solution)/shard_map/convert_element_type | solution.py:68
  215.2 1.6 collective-permute-start
  216.8 93.3 %collective-permute-done = bf16[1,512,4096]{2,1,0:T(8,128)(2,1)S(1)} collective-permute-done((bf16[1,512,4096]{2,1,0:T(8,128)(2,1)}, bf16[1,512,4096]{2,1,0:T(8,128)(2,1)S(1)}, u32[]{:S(2)}, u32[]{:S(2)}) %collective-permute-start) | collective-permute-done | bytes 4194336 | tf_op jit(solution)/shard_map/ppermute | solution.py:15
  310.1 2.0 copy.75
  (27 shorter events, 0.4 us)
Async XLA Ops:
  0.0 1.6 copy-start
  5.9 44.0 %copy-start.6 = (s32[1,16]{1,0:T(1,128)S(1)}, s32[1,16]{1,0:T(1,128)}, u32[]{:S(2)}) copy-start(s32[1,16]{1,0:T(1,128)} %param.15) | copy-start | bytes 196
  5.9 44.6 %copy-start.5 = (s32[1,16,4]{1,2,0:T(4,128)S(1)}, s32[1,16,4]{1,2,0:T(4,128)}, u32[]{:S(2)}) copy-start(s32[1,16,4]{1,2,0:T(4,128)} %param.14) | copy-start | bytes 772
  40.9 41.2 %all-to-all-start.1 = ((bf16[16,128,512]{2,1,0:T(8,128)(2,1)}), bf16[16,128,512]{2,1,0:T(8,128)(2,1)}, u32[]{:S(2)}, u32[]{:S(2)}) async-start(bf16[16,128,512]{2,1,0:T(8,128)(2,1)} %get-tuple-element.95), calls=%async_computation.1 | async-start | bytes 4194304 | tf_op jit(solution)/shard_map/all_to_all | solution.py:98
  50.7 12.7 %copy-start.3 = (bf16[1,512,512]{2,1,0:T(8,128)(2,1)S(1)}, bf16[1,512,512]{2,1,0:T(8,128)(2,1)}, u32[]{:S(2)}) copy-start(bf16[1,512,512]{2,1,0:T(8,128)(2,1)} %param.10) | copy-start | bytes 1572868
  50.7 12.8 %copy-start.4 = (bf16[1,512,512]{2,1,0:T(8,128)(2,1)S(1)}, bf16[1,512,512]{2,1,0:T(8,128)(2,1)}, u32[]{:S(2)}) copy-start(bf16[1,512,512]{2,1,0:T(8,128)(2,1)} %param.11) | copy-start | bytes 1572868
  92.7 3.2 %copy-start.2 = (f32[4,128,512,8]{2,1,3,0:T(8,128)}, f32[4,128,512,8]{2,1,3,0:T(8,128)S(1)}, u32[]{:S(2)}) copy-start(f32[4,128,512,8]{2,1,3,0:T(8,128)S(1)} %get-tuple-element.157) | copy-start | bytes 25165828 | tf_op jit(solution)/shard_map/while
  111.8 3.2 %copy-start.2 = (f32[4,128,512,8]{2,1,3,0:T(8,128)}, f32[4,128,512,8]{2,1,3,0:T(8,128)S(1)}, u32[]{:S(2)}) copy-start(f32[4,128,512,8]{2,1,3,0:T(8,128)S(1)} %get-tuple-element.157) | copy-start | bytes 25165828 | tf_op jit(solution)/shard_map/while
  131.0 3.2 %copy-start.2 = (f32[4,128,512,8]{2,1,3,0:T(8,128)}, f32[4,128,512,8]{2,1,3,0:T(8,128)S(1)}, u32[]{:S(2)}) copy-start(f32[4,128,512,8]{2,1,3,0:T(8,128)S(1)} %get-tuple-element.157) | copy-start | bytes 25165828 | tf_op jit(solution)/shard_map/while
  150.1 3.2 %copy-start.2 = (f32[4,128,512,8]{2,1,3,0:T(8,128)}, f32[4,128,512,8]{2,1,3,0:T(8,128)S(1)}, u32[]{:S(2)}) copy-start(f32[4,128,512,8]{2,1,3,0:T(8,128)S(1)} %get-tuple-element.157) | copy-start | bytes 25165828 | tf_op jit(solution)/shard_map/while
  208.6 103.5 %copy-start.1 = (bf16[1,16,128,512]{3,2,1,0:T(8,128)(2,1)S(1)}, bf16[1,16,128,512]{3,2,1,0:T(8,128)(2,1)}, u32[]{:S(2)}) copy-start(bf16[1,16,128,512]{3,2,1,0:T(8,128)(2,1)} %param.13) | copy-start | bytes 6291460
  215.2 94.9 %collective-permute-start = (bf16[1,512,4096]{2,1,0:T(8,128)(2,1)}, bf16[1,512,4096]{2,1,0:T(8,128)(2,1)S(1)}, u32[]{:S(2)}, u32[]{:S(2)}) collective-permute-start(bf16[1,512,4096]{2,1,0:T(8,128)(2,1)} %copy.37), channel_id=1, source_target_pairs={{112,0},{0,16},{16,32},{32,48},{48,64},{64,80},{80,96},{96,112},{1... | collective-permute-start | bytes 12582920 | tf_op jit(solution)/shard_map/ppermute | solution.py:15
where the time goes:
time: 313 us; the launch traced here: 312 us
  waiting for transfers between devices  93.3 us (30%)
  matrix products  88.8 us (28%)
  local copies, waits for them, and re-layouts  57.6 us (18%)
  blocking collectives  31.7 us (10%)
  other arithmetic  26.6 us (8%)
  starting transfers between devices  10.6 us (3%)
  loops' own time  3.34 us (1%)
    ppermute x1, waiting for transfers between devices, from_behind(): return lax.ppermute(block, axis, route)  93.3 us
    dot_general x5, matrix products, absorb(): jnp.einsum('kgct,tkd->kgcd', weights.astype(jnp.bfloat16), values, prefer...  58.7 us
    all_to_all x1, blocking collectives, shards(): lax.all_to_all(outgoing_keys, 'work', split_axis=0, concat_axis=0, tiled=...  31.7 us
    reduce_sum x5, other arithmetic, absorb(): totals = totals * rescale + jnp.sum(weights, -1)  21.4 us
    dot_general x1, matrix products, local_part(): jnp.einsum('ckgd,tkd->kgct', grouped, own_keys, preferred_element_type=jn...  16.1 us
    while x2, local copies, waits for them, and re-layouts, prefix_part(): return lax.fori_loop(0, prefix_count, visit, state)  14.9 us
    dot_general x4, matrix products, visit(): jnp.einsum('ckgd,tkd->kgct', grouped, key_block, preferred_element_type=j...  14.1 us
    while x12, local copies, waits for them, and re-layouts  12.7 us
  transfers between devices with their start and end apart: 2, of which 1 were waited for; matrix products, arithmetic and copies ran while one was open for 10% of the time, Pallas kernels for 0%

commit v1 on v0

v1 whole, which is shorter than its diff:
```python
import jax
import jax.numpy as jnp
from jax import lax
from jax.experimental import pallas as pl
from jax.experimental.pallas import tpu as pltpu
from jax.sharding import PartitionSpec as P

MESH = pl.DeviceIdType.MESH
HD = 128
BT = 128
MAXB = 4
HELD = 16
C = 512
KVH = 4
GROUP = 8
SECTIONS = 8
Y = 4
NEAR = 2 * Y
TILE = 256
SCALE = HD ** (-0.5) * 1.4426950408889634
EXCLUDED = -1e30


def place():
    work = lax.axis_index("work")
    return lax.axis_index("section"), work // 4, lax.rem(work // 2, 2), lax.rem(work, 2)


def device(section, y, half, core):
    return (lax.rem(section, SECTIONS), (lax.rem(y, Y) * 2 + half) * 2 + core)


def kernel(
    ids, counts, queries, new_keys, new_values, cache_keys, cache_values, out,
    held_keys, held_values, query, keys, values, context, staged, near, pool, picked, far,
    load_sem, query_sem, own_sem, near_sem, pool_sem, far_sem, staged_sem, picked_sem,
    relay_send, relay_recv,
):
    section, y, half, core = place()
    me = (y * 2 + half) * 2 + core
    spot = y * 2 + core
    other_half = 1 - half
    ahead = device(section + 1, y, half, core)
    behind = device(section + SECTIONS - 1, y, half, core)
    across = device(section, y, other_half, core)
    mates = [(y, 1 - core)] + [(lax.rem(y + step, Y), side) for side in (0, 1) for step in (1, 3, 2)]

    loads, query_loads, own_loads = [], [], []
    for g in range(KVH):
        cut = pl.ds(g * HD, HD)
        loads.append([
            pltpu.make_async_copy(cache_keys.at[0, :, :, cut], held_keys[g], load_sem.at[g, 0]),
            pltpu.make_async_copy(cache_values.at[0, :, :, cut], held_values[g], load_sem.at[g, 1]),
        ])
        span = pl.ds(MAXB * BT, C)
        own_loads.append([
            pltpu.make_async_copy(new_keys.at[0, :, cut], keys.at[g, span], own_sem.at[g, 0]),
            pltpu.make_async_copy(new_values.at[0, :, cut], values.at[g, span, pl.ds(0, HD)], own_sem.at[g, 1]),
        ])
        wide = pl.ds(g * GROUP * HD, GROUP * HD)
        query_loads.append(pltpu.make_async_copy(queries.at[0, :, wide], query.at[:, wide], query_sem.at[g]))
    for g in range(KVH):
        for copy in loads[g]:
            copy.start()
    for g in range(KVH):
        for copy in own_loads[g]:
            copy.start()
        query_loads[g].start()

    barrier = pltpu.get_barrier_semaphore()
    greeted = [device(section, my, half, mc) for my, mc in mates] + [ahead, behind, across]
    for other in greeted:
        pl.semaphore_signal(barrier, 1, device_id=other, device_id_type=MESH)

    def listed_here(owner):
        slot = jnp.int32(0)
        for j in range(MAXB):
            offset = ids[0, owner, j] - me * HELD
            hit = (offset >= 0) & (offset < HELD) & (j < counts[0, owner])
            slot = jnp.where(hit, offset, slot)
        return slot

    def holder(owner, j):
        index = lax.shift_right_logical(ids[0, owner, j], 4)
        return (
            lax.shift_right_logical(index, 2) * 2 + (index & 1),
            lax.shift_right_logical(index, 1) & 1,
        )

    slots = [
        (listed_here((my * 2 + other_half) * 2 + mc), listed_here((my * 2 + half) * 2 + mc))
        for my, mc in mates
    ]
    own_slots = (listed_here((y * 2 + other_half) * 2 + core), listed_here(me))

    def sends(g, i):
        my, mc = mates[i]
        to = device(section, my, half, mc)
        return [
            pltpu.make_async_remote_copy(
                src_ref=staged[g].at[i, k],
                dst_ref=(pool, near)[k][g].at[spot],
                send_sem=staged_sem.at[g],
                recv_sem=(pool_sem, near_sem)[k].at[g],
                device_id=to,
                device_id_type=MESH,
            )
            for k in (0, 1)
        ]

    def stage(g):
        for copy in loads[g]:
            copy.wait()
        for i, pair in enumerate(slots):
            for k in (0, 1):
                staged[g][i, k, 0] = held_keys[g][pair[k]]
                staged[g][i, k, 1] = held_values[g][pair[k]]
        for k, buffer in enumerate((pool, near)):
            buffer[g][spot, 0] = held_keys[g][own_slots[k]]
            buffer[g][spot, 1] = held_values[g][own_slots[k]]

    def send_staged(g):
        for i in range(len(mates)):
            for copy in sends(g, i):
                copy.start()

    stage(0)
    pl.semaphore_wait(barrier, len(greeted))
    send_staged(0)
    for g in range(1, KVH):
        stage(g)
        send_staged(g)

    def arrived(buffer, sem, g):
        part = buffer[g].at[pl.ds(0, NEAR - 1)]
        pltpu.make_async_remote_copy(
            src_ref=part, dst_ref=part, send_sem=staged_sem.at[g], recv_sem=sem.at[g],
            device_id=across, device_id_type=MESH,
        ).wait_recv()

    def pass_on(g):
        return pltpu.make_async_remote_copy(
            src_ref=picked[g], dst_ref=far[g], send_sem=picked_sem.at[g], recv_sem=far_sem.at[g],
            device_id=across, device_id_type=MESH,
        )

    def pick(g):
        arrived(pool, pool_sem, g)
        owner = (y * 2 + other_half) * 2 + core
        for j in range(MAXB):
            picked[g][j] = pool[g][holder(owner, j)[0]]
        pass_on(g).start()

    def assemble(g):
        arrived(near, near_sem, g)
        pass_on(g).wait_recv()
        for copy in own_loads[g]:
            copy.wait()
        query_loads[g].wait()
        ones = jnp.ones((BT, HD), jnp.bfloat16)
        first = None
        for j in range(MAXB):
            where, side = holder(me, j)
            block = jnp.where(side == half, near[g][where], far[g][j])
            rows = pl.ds(j * BT, BT)
            if j < MAXB - 1:
                first = block[0] if first is None else first
                keys[g, rows] = block[0]
                values[g, rows, pl.ds(0, HD)] = block[1]
                values[g, rows, pl.ds(HD, HD)] = ones
            else:
                live = j < counts[0, me]
                keys[g, rows] = jnp.where(live, block[0], first)
                values[g, rows, pl.ds(0, HD)] = jnp.where(live, block[1], jnp.zeros_like(block[1]))
                values[g, rows, pl.ds(HD, HD)] = jnp.where(live, ones, jnp.zeros_like(ones))
        values[g, pl.ds(MAXB * BT, C), pl.ds(HD, HD)] = jnp.ones((C, HD), jnp.bfloat16)

    def attend(g, low, high):
        row = lax.broadcasted_iota(jnp.int32, (TILE, TILE), 0)
        column = lax.broadcasted_iota(jnp.int32, (TILE, TILE), 1)
        visible = column <= row

        def head(h, carry):
            cut = pl.ds(pl.multiple_of((g * GROUP + h) * HD, HD), HD)
            for t in range(C // TILE):
                rows = pl.ds(t * TILE, TILE)
                seen = MAXB * BT + (t + 1) * TILE
                scores = lax.dot_general(
                    query[rows, cut], keys[g, pl.ds(0, seen)], (((1,), (1,)), ((), ())),
                    preferred_element_type=jnp.float32,
                )
                last = jnp.where(visible, scores[:, seen - TILE :], EXCLUDED)
                scores = jnp.concatenate([scores[:, : seen - TILE], last], 1)
                peak = jnp.max(scores, 1, keepdims=True)
                weights = jnp.exp2((scores - peak) * SCALE).astype(jnp.bfloat16)
                summed = jnp.dot(weights, values[g, pl.ds(0, seen)], preferred_element_type=jnp.float32)
                context[rows, cut] = (summed[:, :HD] / summed[:, HD:]).astype(jnp.bfloat16)
            pltpu.make_async_remote_copy(
                src_ref=context.at[:, cut], dst_ref=out.at[0, :, cut], send_sem=relay_send, recv_sem=relay_recv,
                device_id=ahead, device_id_type=MESH,
            ).start()
            return carry

        lax.fori_loop(low, high, head, 0)

    pick(0)
    for g in range(KVH):
        assemble(g)
        attend(g, 0, GROUP // 2)
        if g + 1 < KVH:
            pick(g + 1)
        attend(g, GROUP // 2, GROUP)

    for g in range(KVH):
        pltpu.make_async_remote_copy(
            src_ref=staged[g], dst_ref=staged[g], send_sem=staged_sem.at[g], recv_sem=near_sem.at[g],
            device_id=across, device_id_type=MESH,
        ).wait_send()
        pass_on(g).wait_send()
    pltpu.make_async_remote_copy(
        src_ref=context, dst_ref=out.at[0], send_sem=relay_send, recv_sem=relay_recv,
        device_id=ahead, device_id_type=MESH,
    ).wait()


def shards(queries, new_keys, new_values, cache_keys, cache_values, block_ids, block_counts):
    block = (2, BT, HD)
    each = lambda shape: [pltpu.VMEM(shape, jnp.bfloat16)] * KVH
    return pl.pallas_call(
        kernel,
        out_shape=jax.ShapeDtypeStruct(queries.shape, jnp.bfloat16),
        in_specs=[pl.BlockSpec(memory_space=pltpu.SMEM)] * 2 + [pl.BlockSpec(memory_space=pl.ANY)] * 5,
        out_specs=pl.BlockSpec(memory_space=pl.ANY),
        scratch_shapes=[
            each((HELD, BT, HD)),
            each((HELD, BT, HD)),
            pltpu.VMEM((C, KVH * GROUP * HD), jnp.bfloat16),
            pltpu.VMEM((KVH, MAXB * BT + C, HD), jnp.bfloat16),
            pltpu.VMEM((KVH, MAXB * BT + C, 2 * HD), jnp.bfloat16),
            pltpu.VMEM((C, KVH * GROUP * HD), jnp.bfloat16),
            each((NEAR - 1, 2) + block),
            each((NEAR,) + block),
            each((NEAR,) + block),
            each((MAXB,) + block),
            each((MAXB,) + block),
            pltpu.SemaphoreType.DMA((KVH, 2)),
            pltpu.SemaphoreType.DMA((KVH,)),
            pltpu.SemaphoreType.DMA((KVH, 2)),
            pltpu.SemaphoreType.DMA((KVH,)),
            pltpu.SemaphoreType.DMA((KVH,)),
            pltpu.SemaphoreType.DMA((KVH,)),
            pltpu.SemaphoreType.DMA((KVH,)),
            pltpu.SemaphoreType.DMA((KVH,)),
            pltpu.SemaphoreType.DMA,
            pltpu.SemaphoreType.DMA,
        ],
        compiler_params=pltpu.CompilerParams(
            collective_id=0, has_side_effects=True, vmem_limit_bytes=60 * 2**20
        ),
        cost_estimate=pl.CostEstimate(
            flops=4 * 32 * C * (MAXB * BT + C) * HD,
            bytes_accessed=24 * 2**20,
            transcendentals=32 * C * (MAXB * BT + C),
        ),
        name="relayed_attention",
    )(block_ids, block_counts, queries, new_keys, new_values, cache_keys, cache_values)


def solution(mesh):
    in_specs = (
        P("section", "work", None),
        P("section", "work", None),
        P("section", "work", None),
        P("section", "work", None, None),
        P("section", "work", None, None),
        P("section", None, None),
        P("section", None),
    )
    out_specs = P("section", "work", None)
    return jax.shard_map(shards, mesh=mesh, in_specs=in_specs, out_specs=out_specs, check_vma=False)
```

time: 313 us -> 208 us (0.66)
  the two profiles are of different devices: /device:TPU:72 before, /device:TPU:1 now
where the time goes in v1:
time: 208 us; the launch traced here: 205 us
  Pallas kernels  199 us (96%)
  local copies, waits for them, and re-layouts  6.05 us (3%)
    pallas_call x1, Pallas kernels, shards(): pl.pallas_call(kernel, out_shape=jax.ShapeDtypeStruct(queries.shape, jnp....  199 us
    unnamed x2, local copies, waits for them, and re-layouts  6.05 us

profile of v1, /device:TPU:1, one launch (start us, length us, event | category | flops | bytes accessed | tf_op | source)
XLA Modules:
  0.0 205.1 jit_solution(13201605868103053634)
XLA Ops:
  0.0 1.4 copy.8.ids
  1.4 199.0 %relayed_attention.1 = bf16[1,512,4096]{2,1,0:T(8,128)(2,1)} custom-call(s32[1,16,4]{2,1,0:T(8,128)} %copy.8.ids, s32[1,16]{1,0:T(1,128)} %counts.1, bf16[1,512,4096]{2,1,0:T(8,128)(2,1)} %queries.1, bf16[1,512,512]{2,1,0:T(8,128)(2,1)} %new_keys.1, bf16[1,512,512]{2,1,0:T(8,128)(2,1)} %new_values.1, bf16[1,16,128,512]{3,2,1,0:T(8,128)(2,1)} %cache_keys.1, ...), custom_call_target="tpu_custom_call" | custom-call | flops 8589934592 | bytes 25165824 | tf_op jit(solution)/shard_map/relayed_attention/pallas_call | solution.py:229
  200.4 4.7 %copy.10 = bf16[1,512,4096]{2,1,0:T(8,128)(2,1)} copy(bf16[1,512,4096]{2,1,0:T(8,128)(2,1)} %relayed_attention.1) | data formatting | bytes 8388608

commit v2 on v1

--- a/solution.py
+++ b/solution.py
@@ -75,13 +75,13 @@
     def listed_here(owner):
         slot = jnp.int32(0)
         for j in range(MAXB):
-            offset = ids[0, owner, j] - me * HELD
+            offset = ids[0, j, owner] - me * HELD
             hit = (offset >= 0) & (offset < HELD) & (j < counts[0, owner])
             slot = jnp.where(hit, offset, slot)
         return slot
 
     def holder(owner, j):
-        index = lax.shift_right_logical(ids[0, owner, j], 4)
+        index = lax.shift_right_logical(ids[0, j, owner], 4)
         return (
             lax.shift_right_logical(index, 2) * 2 + (index & 1),
             lax.shift_right_logical(index, 1) & 1,
@@ -93,43 +93,35 @@
     ]
     own_slots = (listed_here((y * 2 + other_half) * 2 + core), listed_here(me))
 
-    def sends(g, i):
-        my, mc = mates[i]
-        to = device(section, my, half, mc)
-        return [
+    def stage(g, k):
+        for i, pair in enumerate(slots):
+            staged[g][i, k, 0] = held_keys[g][pair[k]]
+            staged[g][i, k, 1] = held_values[g][pair[k]]
+        buffer = (pool, near)[k][g]
+        buffer[spot, 0] = held_keys[g][own_slots[k]]
+        buffer[spot, 1] = held_values[g][own_slots[k]]
+
+    def send_staged(g, k):
+        for i, (my, mc) in enumerate(mates):
             pltpu.make_async_remote_copy(
                 src_ref=staged[g].at[i, k],
                 dst_ref=(pool, near)[k][g].at[spot],
                 send_sem=staged_sem.at[g],
                 recv_sem=(pool_sem, near_sem)[k].at[g],
-                device_id=to,
+                device_id=device(section, my, half, mc),
                 device_id_type=MESH,
-            )
-            for k in (0, 1)
-        ]
-
-    def stage(g):
+            ).start()
+
+    for g in range(KVH):
         for copy in loads[g]:
             copy.wait()
-        for i, pair in enumerate(slots):
-            for k in (0, 1):
-                staged[g][i, k, 0] = held_keys[g][pair[k]]
-                staged[g][i, k, 1] = held_values[g][pair[k]]
-        for k, buffer in enumerate((pool, near)):
-            buffer[g][spot, 0] = held_keys[g][own_slots[k]]
-            buffer[g][spot, 1] = held_values[g][own_slots[k]]
-
-    def send_staged(g):
-        for i in range(len(mates)):
-            for copy in sends(g, i):
-                copy.start()
-
-    stage(0)
-    pl.semaphore_wait(barrier, len(greeted))
-    send_staged(0)
-    for g in range(1, KVH):
-        stage(g)
-        send_staged(g)
+        stage(g, 0)
+        if g == 0:
+            pl.semaphore_wait(barrier, len(greeted))
+        send_staged(g, 0)
+    for g in range(KVH):
+        stage(g, 1)
+        send_staged(g, 1)
 
     def arrived(buffer, sem, g):
         part = buffer[g].at[pl.ds(0, NEAR - 1)]
@@ -175,7 +167,7 @@
                 values[g, rows, pl.ds(HD, HD)] = jnp.where(live, ones, jnp.zeros_like(ones))
         values[g, pl.ds(MAXB * BT, C), pl.ds(HD, HD)] = jnp.ones((C, HD), jnp.bfloat16)
 
-    def attend(g, low, high):
+    def attend(g):
         row = lax.broadcasted_iota(jnp.int32, (TILE, TILE), 0)
         column = lax.broadcasted_iota(jnp.int32, (TILE, TILE), 1)
         visible = column <= row
@@ -201,15 +193,13 @@
             ).start()
             return carry
 
-        lax.fori_loop(low, high, head, 0)
-
-    pick(0)
+        lax.fori_loop(0, GROUP, head, 0)
+
+    for g in range(KVH):
+        pick(g)
     for g in range(KVH):
         assemble(g)
-        attend(g, 0, GROUP // 2)
-        if g + 1 < KVH:
-            pick(g + 1)
-        attend(g, GROUP // 2, GROUP)
+        attend(g)
 
     for g in range(KVH):
         pltpu.make_async_remote_copy(
@@ -228,9 +218,9 @@
     each = lambda shape: [pltpu.VMEM(shape, jnp.bfloat16)] * KVH
     return pl.pallas_call(
         kernel,
-        out_shape=jax.ShapeDtypeStruct(queries.shape, jnp.bfloat16),
+        out_shape=pltpu.VMEM(queries.shape, jnp.bfloat16),
         in_specs=[pl.BlockSpec(memory_space=pltpu.SMEM)] * 2 + [pl.BlockSpec(memory_space=pl.ANY)] * 5,
-        out_specs=pl.BlockSpec(memory_space=pl.ANY),
+        out_specs=pl.BlockSpec(memory_space=pltpu.VMEM),
         scratch_shapes=[
             each((HELD, BT, HD)),
             each((HELD, BT, HD)),
@@ -255,7 +245,7 @@
             pltpu.SemaphoreType.DMA,
         ],
         compiler_params=pltpu.CompilerParams(
-            collective_id=0, has_side_effects=True, vmem_limit_bytes=60 * 2**20
+            collective_id=0, has_side_effects=True, vmem_limit_bytes=59 * 2**20
         ),
         cost_estimate=pl.CostEstimate(
             flops=4 * 32 * C * (MAXB * BT + C) * HD,
@@ -263,7 +253,7 @@
             transcendentals=32 * C * (MAXB * BT + C),
         ),
         name="relayed_attention",
-    )(block_ids, block_counts, queries, new_keys, new_values, cache_keys, cache_values)
+    )(jnp.swapaxes(block_ids, 1, 2), block_counts, queries, new_keys, new_values, cache_keys, cache_values)
 
 
 def solution(mesh):

time: 208 us -> 134 us (0.64); the launches traced: 205 us -> 134 us
  Pallas kernels: 199 us -> 132 us
  local copies, waits for them, and re-layouts: 6.05 us -> 2.02 us
    pallas_call x1, Pallas kernels: 199 us -> 132 us  [shards(): pl.pallas_call(kernel, out_shape=pltpu.VMEM(queries.shape, jnp.bfloat16),...]
    unnamed x2 -> x1, local copies, waits for them, and re-layouts: 6.05 us -> 2.02 us
where the time goes in v2:
time: 134 us
  Pallas kernels  132 us (99%)
  local copies, waits for them, and re-layouts  2.02 us (2%)
    pallas_call x1, Pallas kernels, shards(): pl.pallas_call(kernel, out_shape=pltpu.VMEM(queries.shape, jnp.bfloat16),...  132 us

profile of v2, /device:TPU:1, one launch (start us, length us, event | category | flops | bytes accessed | tf_op | source)
XLA Modules:
  0.0 134.2 jit_solution(12828366311050917858)
XLA Ops:
  0.0 132.1 %relayed_attention.1 = bf16[1,512,4096]{2,1,0:T(8,128)(2,1)S(1)} custom-call(s32[1,4,16]{2,1,0:T(4,128)} %bitcast.1, s32[1,16]{1,0:T(1,128)} %counts.1, bf16[1,512,4096]{2,1,0:T(8,128)(2,1)} %queries.1, bf16[1,512,512]{2,1,0:T(8,128)(2,1)} %new_keys.1, bf16[1,512,512]{2,1,0:T(8,128)(2,1)} %new_values.1, bf16[1,16,128,512]{3,2,1,0:T(8,128)(2,1)} %cache_keys.1, ...), custom_call_target="tpu_custom_call" | custom-call | flops 8589934592 | bytes 25165824 | tf_op jit(solution)/shard_map/relayed_attention/pallas_call | solution.py:219
  132.1 2.0 %copy.9 = bf16[1,512,4096]{2,1,0:T(8,128)(2,1)} copy(bf16[1,512,4096]{2,1,0:T(8,128)(2,1)S(1)} %relayed_attention.1) | data formatting | bytes 8388608

commit v3 on v2

--- a/solution.py
+++ b/solution.py
@@ -32,8 +32,8 @@
 
 def kernel(
     ids, counts, queries, new_keys, new_values, cache_keys, cache_values, out,
-    held_keys, held_values, query, keys, values, context, staged, near, pool, picked, far,
-    load_sem, query_sem, own_sem, near_sem, pool_sem, far_sem, staged_sem, picked_sem,
+    held_keys, held_values, query, keys, values, context, near_out, far_out, near, pool, picked, far,
+    load_sem, query_sem, own_sem, near_sem, pool_sem, far_sem, near_sent, far_sent, picked_sent,
     relay_send, relay_recv,
 ):
     section, y, half, core = place()
@@ -42,8 +42,11 @@
     other_half = 1 - half
     ahead = device(section + 1, y, half, core)
     behind = device(section + SECTIONS - 1, y, half, core)
-    across = device(section, y, other_half, core)
+    served = lax.rem(y + 1 + 2 * core, Y)
+    server = lax.rem(y + 3 - 2 * core, Y)
+    onward = device(section, served, other_half, core)
     mates = [(y, 1 - core)] + [(lax.rem(y + step, Y), side) for side in (0, 1) for step in (1, 3, 2)]
+    others = [(lax.rem(y + step, Y), side) for side in (0, 1) for step in (0, 1, 3, 2)]
 
     loads, query_loads, own_loads = [], [], []
     for g in range(KVH):
@@ -68,7 +71,8 @@
         query_loads[g].start()
 
     barrier = pltpu.get_barrier_semaphore()
-    greeted = [device(section, my, half, mc) for my, mc in mates] + [ahead, behind, across]
+    greeted = [device(section, my, half, mc) for my, mc in mates] + [ahead, behind]
+    greeted += [device(section, my, other_half, mc) for my, mc in others]
     for other in greeted:
         pl.semaphore_signal(barrier, 1, device_id=other, device_id_type=MESH)
 
@@ -87,65 +91,86 @@
             lax.shift_right_logical(index, 1) & 1,
         )
 
-    slots = [
-        (listed_here((my * 2 + other_half) * 2 + mc), listed_here((my * 2 + half) * 2 + mc))
-        for my, mc in mates
+    def put(target, g, slot):
+        target[0] = held_keys[g][slot]
+        target[1] = held_values[g][slot]
+
+    def send(source, target, sent, arrived, to):
+        pltpu.make_async_remote_copy(
+            src_ref=source, dst_ref=target, send_sem=sent, recv_sem=arrived, device_id=to, device_id_type=MESH
+        ).start()
+
+    near_slots = [listed_here((my * 2 + half) * 2 + mc) for my, mc in mates]
+
+    def stage_near(g):
+        for i, slot in enumerate(near_slots):
+            put(near_out[g].at[i], g, slot)
+        put(near[g].at[spot], g, listed_here(me))
+
+    def send_near(g, chosen):
+        for i in chosen:
+            my, mc = mates[i]
+            send(near_out[g].at[i], near[g].at[spot], near_sent.at[g], near_sem.at[g], device(section, my, half, mc))
+
+    def stage_pool(g):
+        for i, slot in enumerate(pool_slots):
+            put(far_out[g].at[i], g, slot)
+        put(pool[g].at[spot], g, listed_here((served * 2 + other_half) * 2 + core))
+
+    def send_pool(g):
+        for i, (my, mc) in enumerate(mates):
+            send(far_out[g].at[i], pool[g].at[spot], far_sent.at[g], pool_sem.at[g], device(section, my, half, mc))
+
+    for copy in loads[0]:
+        copy.wait()
+    stage_near(0)
+    for i, (my, mc) in enumerate(others):
+        put(far_out[0].at[i], 0, listed_here((my * 2 + other_half) * 2 + mc))
+    pl.semaphore_wait(barrier, len(greeted))
+    send_near(0, [0])
+    for side in (0, 1):
+        send_near(0, range(1 + 3 * side, 4 + 3 * side))
+        for i in range(4 * side, 4 * side + 4):
+            my, mc = others[i]
+            send(
+                far_out[0].at[i], far[0].at[spot], far_sent.at[0], far_sem.at[0],
+                device(section, my, other_half, mc),
+            )
+
+    pool_slots = [
+        listed_here((lax.rem(my + 1 + 2 * mc, Y) * 2 + other_half) * 2 + mc) for my, mc in mates
     ]
-    own_slots = (listed_here((y * 2 + other_half) * 2 + core), listed_here(me))
-
-    def stage(g, k):
-        for i, pair in enumerate(slots):
-            staged[g][i, k, 0] = held_keys[g][pair[k]]
-            staged[g][i, k, 1] = held_values[g][pair[k]]
-        buffer = (pool, near)[k][g]
-        buffer[spot, 0] = held_keys[g][own_slots[k]]
-        buffer[spot, 1] = held_values[g][own_slots[k]]
-
-    def send_staged(g, k):
-        for i, (my, mc) in enumerate(mates):
-            pltpu.make_async_remote_copy(
-                src_ref=staged[g].at[i, k],
-                dst_ref=(pool, near)[k][g].at[spot],
-                send_sem=staged_sem.at[g],
-                recv_sem=(pool_sem, near_sem)[k].at[g],
-                device_id=device(section, my, half, mc),
-                device_id_type=MESH,
-            ).start()
-
-    for g in range(KVH):
+
+    def exchange(g):
         for copy in loads[g]:
             copy.wait()
-        stage(g, 0)
-        if g == 0:
-            pl.semaphore_wait(barrier, len(greeted))
-        send_staged(g, 0)
-    for g in range(KVH):
-        stage(g, 1)
-        send_staged(g, 1)
-
-    def arrived(buffer, sem, g):
-        part = buffer[g].at[pl.ds(0, NEAR - 1)]
+        stage_pool(g)
+        send_pool(g)
+        stage_near(g)
+        send_near(g, range(len(mates)))
+
+    exchange(1)
+
+    def arrived(part, sem):
         pltpu.make_async_remote_copy(
-            src_ref=part, dst_ref=part, send_sem=staged_sem.at[g], recv_sem=sem.at[g],
-            device_id=across, device_id_type=MESH,
+            src_ref=part, dst_ref=part, send_sem=far_sent.at[0], recv_sem=sem, device_id=ahead, device_id_type=MESH
         ).wait_recv()
 
-    def pass_on(g):
-        return pltpu.make_async_remote_copy(
-            src_ref=picked[g], dst_ref=far[g], send_sem=picked_sem.at[g], recv_sem=far_sem.at[g],
-            device_id=across, device_id_type=MESH,
-        )
+    def left(part, sem):
+        pltpu.make_async_remote_copy(
+            src_ref=part, dst_ref=part, send_sem=sem, recv_sem=far_sem.at[0], device_id=ahead, device_id_type=MESH
+        ).wait_send()
 
     def pick(g):
-        arrived(pool, pool_sem, g)
-        owner = (y * 2 + other_half) * 2 + core
+        arrived(pool[g].at[pl.ds(0, NEAR - 1)], pool_sem.at[g])
+        owner = (served * 2 + other_half) * 2 + core
         for j in range(MAXB):
             picked[g][j] = pool[g][holder(owner, j)[0]]
-        pass_on(g).start()
+        send(picked[g], far[g], picked_sent.at[g], far_sem.at[g], onward)
 
     def assemble(g):
-        arrived(near, near_sem, g)
-        pass_on(g).wait_recv()
+        arrived(near[g].at[pl.ds(0, NEAR - 1)], near_sem.at[g])
+        arrived(far[g], far_sem.at[g])
         for copy in own_loads[g]:
             copy.wait()
         query_loads[g].wait()
@@ -153,7 +178,7 @@
         first = None
         for j in range(MAXB):
             where, side = holder(me, j)
-            block = jnp.where(side == half, near[g][where], far[g][j])
+            block = jnp.where(side == half, near[g][where], far[g][where if g == 0 else j])
             rows = pl.ds(j * BT, BT)
             if j < MAXB - 1:
                 first = block[0] if first is None else first
@@ -196,17 +221,18 @@
         lax.fori_loop(0, GROUP, head, 0)
 
     for g in range(KVH):
-        pick(g)
-    for g in range(KVH):
         assemble(g)
         attend(g)
-
-    for g in range(KVH):
-        pltpu.make_async_remote_copy(
-            src_ref=staged[g], dst_ref=staged[g], send_sem=staged_sem.at[g], recv_sem=near_sem.at[g],
-            device_id=across, device_id_type=MESH,
-        ).wait_send()
-        pass_on(g).wait_send()
+        if g + 1 < KVH:
+            pick(g + 1)
+        if g + 2 < KVH:
+            exchange(g + 2)
+
+    for g in range(KVH):
+        left(near_out[g], near_sent.at[g])
+        left(far_out[g], far_sent.at[g])
+        if g > 0:
+            left(picked[g], picked_sent.at[g])
     pltpu.make_async_remote_copy(
         src_ref=context, dst_ref=out.at[0], send_sem=relay_send, recv_sem=relay_recv,
         device_id=ahead, device_id_type=MESH,
@@ -216,6 +242,7 @@
 def shards(queries, new_keys, new_values, cache_keys, cache_values, block_ids, block_counts):
     block = (2, BT, HD)
     each = lambda shape: [pltpu.VMEM(shape, jnp.bfloat16)] * KVH
+    first_and = lambda one, rest: [pltpu.VMEM(one, jnp.bfloat16)] + [pltpu.VMEM(rest, jnp.bfloat16)] * (KVH - 1)
     return pl.pallas_call(
         kernel,
         out_shape=pltpu.VMEM(queries.shape, jnp.bfloat16),
@@ -228,14 +255,16 @@
             pltpu.VMEM((KVH, MAXB * BT + C, HD), jnp.bfloat16),
             pltpu.VMEM((KVH, MAXB * BT + C, 2 * HD), jnp.bfloat16),
             pltpu.VMEM((C, KVH * GROUP * HD), jnp.bfloat16),
-            each((NEAR - 1, 2) + block),
+            each((NEAR - 1,) + block),
+            first_and((NEAR,) + block, (NEAR - 1,) + block),
             each((NEAR,) + block),
-            each((NEAR,) + block),
-            each((MAXB,) + block),
-            each((MAXB,) + block),
+            first_and((1,) + block, (NEAR,) + block),
+            first_and((1,) + block, (MAXB,) + block),
+            first_and((NEAR,) + block, (MAXB,) + block),
             pltpu.SemaphoreType.DMA((KVH, 2)),
             pltpu.SemaphoreType.DMA((KVH,)),
             pltpu.SemaphoreType.DMA((KVH, 2)),
+            pltpu.SemaphoreType.DMA((KVH,)),
             pltpu.SemaphoreType.DMA((KVH,)),
             pltpu.SemaphoreType.DMA((KVH,)),
             pltpu.SemaphoreType.DMA((KVH,)),

time: 134 us -> 132 us (0.985)
  Pallas kernels: 132 us -> 130 us
    pallas_call x1, Pallas kernels: 132 us -> 130 us  [shards(): pl.pallas_call(kernel, out_shape=pltpu.VMEM(queries.shape, jnp.bfloat16),...]
where the time goes in v3:
time: 132 us
  Pallas kernels  130 us (98%)
  local copies, waits for them, and re-layouts  2.02 us (2%)
    pallas_call x1, Pallas kernels, shards(): pl.pallas_call(kernel, out_shape=pltpu.VMEM(queries.shape, jnp.bfloat16),...  130 us

profile of v3, /device:TPU:1, one launch (start us, length us, event | category | flops | bytes accessed | tf_op | source)
XLA Modules:
  0.0 131.8 jit_solution(18133471456299279139)
XLA Ops:
  0.0 129.8 %relayed_attention.1 = bf16[1,512,4096]{2,1,0:T(8,128)(2,1)S(1)} custom-call(s32[1,4,16]{2,1,0:T(4,128)} %bitcast.1, s32[1,16]{1,0:T(1,128)} %counts.1, bf16[1,512,4096]{2,1,0:T(8,128)(2,1)} %queries.1, bf16[1,512,512]{2,1,0:T(8,128)(2,1)} %new_keys.1, bf16[1,512,512]{2,1,0:T(8,128)(2,1)} %new_values.1, bf16[1,16,128,512]{3,2,1,0:T(8,128)(2,1)} %cache_keys.1, ...), custom_call_target="tpu_custom_call" | custom-call | flops 8589934592 | bytes 25165824 | tf_op jit(solution)/shard_map/relayed_attention/pallas_call | solution.py:246
  129.8 2.0 %copy.9 = bf16[1,512,4096]{2,1,0:T(8,128)(2,1)} copy(bf16[1,512,4096]{2,1,0:T(8,128)(2,1)S(1)} %relayed_attention.1) | data formatting | bytes 8388608

commit v4 on v3

--- a/solution.py
+++ b/solution.py
@@ -31,9 +31,9 @@
 
 
 def kernel(
-    ids, counts, queries, new_keys, new_values, cache_keys, cache_values, out,
-    held_keys, held_values, query, keys, values, context, near_out, far_out, near, pool, picked, far,
-    load_sem, query_sem, own_sem, near_sem, pool_sem, far_sem, near_sent, far_sent, picked_sent,
+    all_ids, all_counts, queries, new_keys, new_values, cache_keys, cache_values, out,
+    ids, counts, held_keys, held_values, query, keys, values, context, near_out, far_out, near, pool, picked, far,
+    list_sem, load_sem, query_sem, own_sem, near_sem, pool_sem, far_sem, near_sent, far_sent, picked_sent,
     relay_send, relay_recv,
 ):
     section, y, half, core = place()
@@ -62,19 +62,21 @@
         ])
         wide = pl.ds(g * GROUP * HD, GROUP * HD)
         query_loads.append(pltpu.make_async_copy(queries.at[0, :, wide], query.at[:, wide], query_sem.at[g]))
-    for g in range(KVH):
-        for copy in loads[g]:
-            copy.start()
-    for g in range(KVH):
-        for copy in own_loads[g]:
-            copy.start()
-        query_loads[g].start()
+    lists = [
+        pltpu.make_async_copy(all_ids, ids, list_sem.at[0]),
+        pltpu.make_async_copy(all_counts, counts, list_sem.at[1]),
+    ]
+    for copy in lists + loads[0]:
+        copy.start()
 
     barrier = pltpu.get_barrier_semaphore()
     greeted = [device(section, my, half, mc) for my, mc in mates] + [ahead, behind]
     greeted += [device(section, my, other_half, mc) for my, mc in others]
     for other in greeted:
         pl.semaphore_signal(barrier, 1, device_id=other, device_id_type=MESH)
+
+    for copy in lists:
+        copy.wait()
 
     def listed_here(owner):
         slot = jnp.int32(0)
@@ -105,7 +107,7 @@
     def stage_near(g):
         for i, slot in enumerate(near_slots):
             put(near_out[g].at[i], g, slot)
-        put(near[g].at[spot], g, listed_here(me))
+        put(near[g].at[spot], g, own_slot)
 
     def send_near(g, chosen):
         for i in chosen:
@@ -121,22 +123,31 @@
         for i, (my, mc) in enumerate(mates):
             send(far_out[g].at[i], pool[g].at[spot], far_sent.at[g], pool_sem.at[g], device(section, my, half, mc))
 
+    far_slots = [listed_here((my * 2 + other_half) * 2 + mc) for my, mc in others]
+    own_slot = listed_here(me)
     for copy in loads[0]:
         copy.wait()
+    for copy in loads[1] + own_loads[0] + [query_loads[0]]:
+        copy.start()
+    for i, slot in enumerate(far_slots):
+        put(far_out[0].at[i], 0, slot)
     stage_near(0)
-    for i, (my, mc) in enumerate(others):
-        put(far_out[0].at[i], 0, listed_here((my * 2 + other_half) * 2 + mc))
     pl.semaphore_wait(barrier, len(greeted))
-    send_near(0, [0])
-    for side in (0, 1):
-        send_near(0, range(1 + 3 * side, 4 + 3 * side))
-        for i in range(4 * side, 4 * side + 4):
+    def send_far(chosen):
+        for i in chosen:
             my, mc = others[i]
             send(
                 far_out[0].at[i], far[0].at[spot], far_sent.at[0], far_sem.at[0],
                 device(section, my, other_half, mc),
             )
 
+    send_near(0, [0])
+    send_far((3, 1, 2, 0))
+    send_near(0, (3, 1, 2, 4, 5, 6))
+    send_far((4, 5, 6, 7))
+    for g in range(1, KVH):
+        for copy in (loads[g + 1] if g + 1 < KVH else []) + own_loads[g] + [query_loads[g]]:
+            copy.start()
     pool_slots = [
         listed_here((lax.rem(my + 1 + 2 * mc, Y) * 2 + other_half) * 2 + mc) for my, mc in mates
     ]
@@ -148,8 +159,6 @@
         send_pool(g)
         stage_near(g)
         send_near(g, range(len(mates)))
-
-    exchange(1)
 
     def arrived(part, sem):
         pltpu.make_async_remote_copy(
@@ -212,16 +221,15 @@
                 weights = jnp.exp2((scores - peak) * SCALE).astype(jnp.bfloat16)
                 summed = jnp.dot(weights, values[g, pl.ds(0, seen)], preferred_element_type=jnp.float32)
                 context[rows, cut] = (summed[:, :HD] / summed[:, HD:]).astype(jnp.bfloat16)
-            pltpu.make_async_remote_copy(
-                src_ref=context.at[:, cut], dst_ref=out.at[0, :, cut], send_sem=relay_send, recv_sem=relay_recv,
-                device_id=ahead, device_id_type=MESH,
-            ).start()
+                send(context.at[rows, cut], out.at[0, rows, cut], relay_send, relay_recv, ahead)
             return carry
 
         lax.fori_loop(0, GROUP, head, 0)
 
     for g in range(KVH):
         assemble(g)
+        if g == 0:
+            exchange(1)
         attend(g)
         if g + 1 < KVH:
             pick(g + 1)
@@ -246,9 +254,11 @@
     return pl.pallas_call(
         kernel,
         out_shape=pltpu.VMEM(queries.shape, jnp.bfloat16),
-        in_specs=[pl.BlockSpec(memory_space=pltpu.SMEM)] * 2 + [pl.BlockSpec(memory_space=pl.ANY)] * 5,
+        in_specs=[pl.BlockSpec(memory_space=pl.ANY)] * 7,
         out_specs=pl.BlockSpec(memory_space=pltpu.VMEM),
         scratch_shapes=[
+            pltpu.SMEM((1,) + (MAXB, block_ids.shape[1]), jnp.int32),
+            pltpu.SMEM(block_counts.shape, jnp.int32),
             each((HELD, BT, HD)),
             each((HELD, BT, HD)),
             pltpu.VMEM((C, KVH * GROUP * HD), jnp.bfloat16),
@@ -261,6 +271,7 @@
             first_and((1,) + block, (NEAR,) + block),
             first_and((1,) + block, (MAXB,) + block),
             first_and((NEAR,) + block, (MAXB,) + block),
+            pltpu.SemaphoreType.DMA((2,)),
             pltpu.SemaphoreType.DMA((KVH, 2)),
             pltpu.SemaphoreType.DMA((KVH,)),
             pltpu.SemaphoreType.DMA((KVH, 2)),

time: 132 us -> 131 us (level)
  no operation moved by 1% of the time
where the time goes in v4:
time: 131 us
  Pallas kernels  129 us (98%)
  local copies, waits for them, and re-layouts  2.02 us (2%)
    pallas_call x1, Pallas kernels, shards(): pl.pallas_call(kernel, out_shape=pltpu.VMEM(queries.shape, jnp.bfloat16),...  129 us

profile of v4, /device:TPU:1, one launch (start us, length us, event | category | flops | bytes accessed | tf_op | source)
XLA Modules:
  0.0 131.0 jit_solution(7203285252957252188)
XLA Ops:
  0.0 129.0 %relayed_attention.1 = bf16[1,512,4096]{2,1,0:T(8,128)(2,1)S(1)} custom-call(s32[1,4,16]{2,1,0:T(4,128)} %bitcast.1, s32[1,16]{1,0:T(1,128)} %all_counts.1, bf16[1,512,4096]{2,1,0:T(8,128)(2,1)} %queries.1, bf16[1,512,512]{2,1,0:T(8,128)(2,1)} %new_keys.1, bf16[1,512,512]{2,1,0:T(8,128)(2,1)} %new_values.1, bf16[1,16,128,512]{3,2,1,0:T(8,128)(2,1)} %cache_keys.1, ...), custom_call_target="tpu_custom_call" | custom-call | flops 8589934592 | bytes 25165824 | tf_op jit(solution)/shard_map/relayed_attention/pallas_call | solution.py:254
  129.0 2.0 %copy.9 = bf16[1,512,4096]{2,1,0:T(8,128)(2,1)} copy(bf16[1,512,4096]{2,1,0:T(8,128)(2,1)S(1)} %relayed_attention.1) | data formatting | bytes 8388608

commit v5 on v4

--- a/solution.py
+++ b/solution.py
@@ -141,10 +141,9 @@
                 device(section, my, other_half, mc),
             )
 
-    send_near(0, [0])
-    send_far((3, 1, 2, 0))
-    send_near(0, (3, 1, 2, 4, 5, 6))
-    send_far((4, 5, 6, 7))
+    send_far((0, 4, 3, 1, 2))
+    send_near(0, (0, 3, 1, 2, 4, 5, 6))
+    send_far((5, 6, 7))
     for g in range(1, KVH):
         for copy in (loads[g + 1] if g + 1 < KVH else []) + own_loads[g] + [query_loads[g]]:
             copy.start()

time: 131 us -> 131 us (level)
  no operation moved by 1% of the time
where the time goes in v5:
time: 131 us
  Pallas kernels  129 us (98%)
  local copies, waits for them, and re-layouts  2.02 us (2%)
    pallas_call x1, Pallas kernels, shards(): pl.pallas_call(kernel, out_shape=pltpu.VMEM(queries.shape, jnp.bfloat16),...  129 us

profile of v5, /device:TPU:1, one launch (start us, length us, event | category | flops | bytes accessed | tf_op | source)
XLA Modules:
  0.0 131.0 jit_solution(9257137557303646576)
XLA Ops:
  0.0 129.0 %relayed_attention.1 = bf16[1,512,4096]{2,1,0:T(8,128)(2,1)S(1)} custom-call(s32[1,4,16]{2,1,0:T(4,128)} %bitcast.1, s32[1,16]{1,0:T(1,128)} %all_counts.1, bf16[1,512,4096]{2,1,0:T(8,128)(2,1)} %queries.1, bf16[1,512,512]{2,1,0:T(8,128)(2,1)} %new_keys.1, bf16[1,512,512]{2,1,0:T(8,128)(2,1)} %new_values.1, bf16[1,16,128,512]{3,2,1,0:T(8,128)(2,1)} %cache_keys.1, ...), custom_call_target="tpu_custom_call" | custom-call | flops 8589934592 | bytes 25165824 | tf_op jit(solution)/shard_map/relayed_attention/pallas_call | solution.py:253
  129.0 2.0 %copy.9 = bf16[1,512,4096]{2,1,0:T(8,128)(2,1)} copy(bf16[1,512,4096]{2,1,0:T(8,128)(2,1)S(1)} %relayed_attention.1) | data formatting | bytes 8388608
